TPU v7x, 512 devices: a whole 4x4x16 slice. The times are simulated.
512 devices in a mesh: gx: 16 (over x, y), gy: 32 (over z, core).
Axes of the slice: x: 4, y: 4, z: 16, core: 2. Of those that a mesh axis runs over, the one named last changes fastest.
Arguments:
- residual: bfloat16 [64, 6144], P('gy', 'gx')
- attn_gain: float32 [6144], P('gx'), may hold values from 0.25 to 1.75
- wqkv: bfloat16 [6144, 8192], P('gx', 'gy'), may hold values from -0.078125 to 0.078125
- rotated_key_cache: bfloat16 [64, 2048, 1024], P('gx', 'gy'), may hold values from -6 to 6
- slot_value_cache: bfloat16 [64, 2048, 1024], P('gx', 'gy'), may hold values from -6 to 6
- lengths: int32 [64], P('gx'), may hold values from 0 to 8191
- starts: int32 [64], P('gx'), may hold values from 0 to 8191, as said below
- wo: bfloat16 [6144, 6144], P('gy', 'gx')
- post_gain: float32 [6144], P('gx'), may hold values from 0.25 to 1.75
- moe_gain: float32 [6144], P('gx'), may hold values from 0.25 to 1.75
- router: bfloat16 [6144, 8], P('gx'), may hold values from -0.15625 to 0.15625
- expert_ids: int32 [64, 2], replicated, may hold values from 0 to 7, all different within a row; in each aligned block of 64 rows (0 to 63, 64 to 127, ...) at most 32 rows name the same one
- w_gate_up: bfloat16 [2, 6144, 2, 16384], P(None, 'gx', None, 'gy'), may hold values from -0.078125 to 0.078125
- w_down: bfloat16 [2, 16384, 6144], P(None, 'gy', 'gx'), may hold values from -0.1875 to 0.1875
Outputs:
- mixed: bfloat16 [64, 6144], P('gy', 'gx')
- expert_out: bfloat16 [64, 6144], P('gy', 'gx')
Inputs may be any that keep to these rules, and one draw needn't show every extreme that they name: `starts`: each start is at most its request's length. `expert_ids`: the 2 experts of a request differ; no expert is named by more than 32 requests, a bound that some block reaches.
All inputs are finite; a program needn't handle non-finite values.
Results may differ from a plain program's by a relative error of at most 0.025.
Values may be sent and summed in bfloat16 or wider, within the bound.
A program may use at most 64 MiB of HBM per device.

v0:
```python
import jax
import jax.numpy as jnp
from jax import lax
from jax.sharding import PartitionSpec as P

MODEL_WIDTH = 6144
QUERY_HEADS = 48
KEY_VALUE_HEADS = 8
HEAD_SIZE = 128
WINDOW_SLOTS = 2048
EXP_WIN = 2


epsilon = 1e-05
score_cap = 30.0


def rotary_position_rotate(blocks, positions):
    half_width = blocks.shape[-1] // 2
    frequency = 10000.0 ** (-(jnp.arange(half_width, dtype=jnp.float32) * 2.0 / blocks.shape[-1]))
    angles = positions.astype(jnp.float32)[:, None] * frequency[None, :]
    cosine = jnp.cos(angles)[:, None, :]
    sine_part = jnp.sin(angles)[:, None, :]
    leading = blocks[..., :half_width]
    trailing = blocks[..., half_width:]
    return jnp.concatenate(
        [leading * cosine - trailing * sine_part, trailing * cosine + leading * sine_part], axis=-1
    )


def input_scale(values):
    squares = lax.psum(jnp.sum(values * values, axis=-1), "gx")
    return lax.rsqrt(squares / MODEL_WIDTH + epsilon)[:, None]


def combine_weights(id_rows, chances):
    window = jnp.arange(EXP_WIN, dtype=jnp.int32)
    chosen = jnp.any(id_rows[:, :, None] == window[None, None, :], axis=1)
    return jnp.where(chosen, chances[:, :EXP_WIN], 0.0).astype(jnp.bfloat16)


def local(
    residual,
    attn_gain,
    wqkv,
    rotated_key_cache,
    slot_value_cache,
    lengths,
    starts,
    wo,
    post_gain,
    moe_gain,
    router,
    expert_ids,
    w_gate_up,
    w_down,
):
    rows_gy = residual.shape[0]
    gy_count = lax.axis_size("gy")
    gx_count = lax.axis_size("gx")
    all_rows = rows_gy * gy_count
    rows_per_column_group = all_rows // gx_count
    gy_index = lax.axis_index("gy")
    own_first = gy_index * rows_gy
    base_rows = residual.astype(jnp.float32)
    normed = (base_rows * input_scale(base_rows) * attn_gain).astype(jnp.bfloat16)
    normed_all = lax.all_gather(normed, "gy", axis=0, tiled=True)
    slab_rows = normed_all
    query_key_value_sums = lax.psum_scatter(
        jnp.dot(slab_rows, wqkv, preferred_element_type=jnp.float32),
        "gx",
        scatter_dimension=0,
        tiled=True,
    )
    heads_here = wqkv.shape[1] // HEAD_SIZE
    head_block_list = query_key_value_sums.reshape(rows_per_column_group, heads_here, HEAD_SIZE)
    global_head_index = gy_index * heads_here + jnp.arange(heads_here, dtype=jnp.int32)
    rotary_angles = (global_head_index < QUERY_HEADS + KEY_VALUE_HEADS)[None, :, None]
    head_block_list = jnp.where(
        rotary_angles, rotary_position_rotate(head_block_list, lengths), head_block_list
    )
    head_slab = head_block_list.reshape(rows_per_column_group, heads_here * HEAD_SIZE).astype(
        jnp.bfloat16
    )
    query_key_value_rows = lax.all_gather(head_slab, "gy", axis=1, tiled=True)
    query_group_width = QUERY_HEADS // KEY_VALUE_HEADS
    logit_scale_factor = HEAD_SIZE ** (-0.5)
    query_rows = query_key_value_rows[:, : QUERY_HEADS * HEAD_SIZE].reshape(
        rows_per_column_group, KEY_VALUE_HEADS, query_group_width, HEAD_SIZE
    )
    fresh_key = query_key_value_rows[
        :, QUERY_HEADS * HEAD_SIZE : (QUERY_HEADS + KEY_VALUE_HEADS) * HEAD_SIZE
    ].reshape(rows_per_column_group, KEY_VALUE_HEADS, HEAD_SIZE)
    fresh_value = query_key_value_rows[:, (QUERY_HEADS + KEY_VALUE_HEADS) * HEAD_SIZE :].reshape(
        rows_per_column_group, KEY_VALUE_HEADS, HEAD_SIZE
    )
    local_slots = rotated_key_cache.shape[1]
    local_keys = rotated_key_cache.reshape(
        rows_per_column_group, local_slots, KEY_VALUE_HEADS, HEAD_SIZE
    )
    local_values = slot_value_cache.reshape(
        rows_per_column_group, local_slots, KEY_VALUE_HEADS, HEAD_SIZE
    )
    scores = (
        jnp.einsum("rhgd,rshd->rhgs", query_rows, local_keys, preferred_element_type=jnp.float32)
        * logit_scale_factor
    )
    scores = score_cap * jnp.tanh(scores / score_cap)
    slot_index = gy_index * local_slots + jnp.arange(local_slots, dtype=jnp.int32)
    latest = (lengths - 1)[:, None]
    position = latest - jnp.mod(latest - slot_index[None, :], WINDOW_SLOTS)
    lowest = jnp.maximum(starts, lengths - WINDOW_SLOTS + 1)[:, None]
    usable = position >= lowest
    weights = jnp.where(usable[:, None, None, :], jnp.exp(scores), 0.0)
    weighted_value_sum = jnp.einsum(
        "rhgs,rshd->rhgd",
        weights.astype(jnp.bfloat16),
        local_values,
        preferred_element_type=jnp.float32,
    )
    denominator = jnp.sum(weights, axis=-1)
    weighted_value_sum, denominator = lax.psum((weighted_value_sum, denominator), "gy")
    self_score = (
        jnp.einsum("rhgd,rhd->rhg", query_rows, fresh_key, preferred_element_type=jnp.float32)
        * logit_scale_factor
    )
    own_weight = jnp.exp(score_cap * jnp.tanh(self_score / score_cap))
    weighted_value_sum = weighted_value_sum + jnp.einsum(
        "rhg,rhd->rhgd",
        own_weight.astype(jnp.bfloat16),
        fresh_value,
        preferred_element_type=jnp.float32,
    )
    denominator = denominator + own_weight
    attended = (
        (weighted_value_sum / denominator[..., None])
        .reshape(rows_per_column_group, QUERY_HEADS * HEAD_SIZE)
        .astype(jnp.bfloat16)
    )
    feature_count = wo.shape[0]
    my_features = lax.dynamic_slice_in_dim(attended, gy_index * feature_count, feature_count, 1)
    out_partial = jnp.dot(
        lax.all_gather(my_features, "gx", axis=0, tiled=True),
        wo,
        preferred_element_type=jnp.float32,
    )
    branch = lax.psum_scatter(out_partial, "gy", scatter_dimension=0, tiled=True)
    gained = branch * post_gain
    router_wide = router.astype(jnp.float32)
    branch_sq = lax.psum(jnp.sum(branch * branch, axis=-1), "gx")
    post_scale = lax.rsqrt(branch_sq / MODEL_WIDTH + epsilon)[:, None]
    stream_mid = base_rows + post_scale * gained
    stream_sq, router_part = lax.psum(
        (
            jnp.sum(stream_mid * stream_mid, axis=-1),
            jnp.dot(stream_mid * moe_gain, router_wide, precision=lax.Precision.HIGHEST),
        ),
        "gx",
    )
    pre_scale = lax.rsqrt(stream_sq / MODEL_WIDTH + epsilon)[:, None]
    logits = router_part * pre_scale
    exponent = jnp.exp(logits)
    chances = exponent / jnp.sum(exponent, axis=-1, keepdims=True)
    moe_input = (stream_mid * pre_scale * moe_gain).astype(jnp.bfloat16)
    id_rows = lax.dynamic_slice_in_dim(expert_ids, own_first, rows_gy, 0)
    combine = combine_weights(id_rows, chances)
    moe_all, combine_all = (
        lax.all_gather(moe_input, "gy", axis=0, tiled=True),
        lax.all_gather(combine, "gy", axis=0, tiled=True),
    )
    capacity = all_rows // 2
    window = jnp.arange(EXP_WIN, dtype=jnp.int32)
    picked = jnp.any(expert_ids[:, :, None] == window[None, None, :], axis=1).astype(jnp.int32)
    slot_of = jnp.cumsum(picked, axis=0) - 1
    slot_ids = jnp.arange(capacity, dtype=jnp.int32)
    placing = (slot_of.T[:, None, :] == slot_ids[None, :, None]) & (picked.T[:, None, :] == 1)
    source = jnp.einsum(
        "eqr,rx->qex", placing.astype(jnp.bfloat16), moe_all, preferred_element_type=jnp.float32
    ).astype(jnp.bfloat16)
    slab_rows = source
    gate_up = lax.psum(
        jnp.einsum("qex,exuf->qeuf", slab_rows, w_gate_up, preferred_element_type=jnp.float32), "gx"
    )
    hidden = (jax.nn.gelu(gate_up[:, :, 0], approximate=True) * gate_up[:, :, 1]).astype(
        jnp.bfloat16
    )
    expert_terms = jnp.einsum("ref,efx->rex", hidden, w_down, preferred_element_type=jnp.float32)
    placed = jnp.einsum(
        "eqr,qex->rex", placing.astype(jnp.float32), expert_terms, precision=lax.Precision.HIGHEST
    )
    weighted = jnp.sum(placed * combine_all.astype(jnp.float32)[:, :, None], axis=1)
    expert_out = lax.psum_scatter(weighted, "gy", scatter_dimension=0, tiled=True)
    return (stream_mid.astype(jnp.bfloat16), expert_out.astype(jnp.bfloat16))


def solution(mesh):
    return jax.shard_map(
        local,
        mesh=mesh,
        in_specs=(
            P("gy", "gx"),
            P("gx"),
            P("gx", "gy"),
            P("gx", "gy", None),
            P("gx", "gy", None),
            P("gx"),
            P("gx"),
            P("gy", "gx"),
            P("gx"),
            P("gx"),
            P("gx", None),
            P(),
            P(None, "gx", None, "gy"),
            P(None, "gy", "gx"),
        ),
        out_specs=(P("gy", "gx"), P("gy", "gx")),
        check_vma=False,
    )
```

profile of v0, /device:TPU:1, one launch (start us, length us, event | category | flops | bytes accessed | tf_op | source)
XLA Modules:
  0.0 1029.8 jit_solution(17580553421535568091)
XLA Ops:
  7.2 0.9 fusion.46
  8.2 34.2 %psum.49 = f32[2]{0:T(128)S(1)} all-reduce(f32[2]{0:T(128)S(1)} %fusion.46), channel_id=1, replica_groups=mesh['gx'=16,'gy'=32] {'gx'}, use_global_device_ids=true, to_apply=%region_1.0 | all-reduce | flops 2 | bytes 16 | tf_op jit(solution)/shard_map/psum | solution.py:32
  42.4 0.8 fusion.55
  43.2 44.1 %all-gather = bf16[32,2,384]{2,1,0:T(2,128)(2,1)S(1)} all-gather(bf16[1,2,384]{2,1,0:T(2,128)(2,1)S(1)} %fusion.55), channel_id=1, replica_groups=mesh['gx'=16,'gy'=32] {'gy'}, dimensions={0}, use_global_device_ids=true | all-gather | bytes 50688 | tf_op jit(solution)/shard_map/all_gather | solution.py:67
  87.3 1.7 fusion.65
  89.2 0.7 compare_reduce_fusion.1
  89.9 0.1 copy.53
  90.0 0.1 reduce_window_sum.11
  90.1 0.7 broadcast_add_fusion
  90.9 0.1 multiply_cosine_fusion
  91.1 0.8 constant_dynamic-slice_fusion.1
  91.8 0.1 copy.57
  91.9 1.3 dynamic-slice
  93.8 95.9 %all-reduce.13.cloned.1.call-done = f32[64,256]{1,0:T(8,128)} async-done(((f32[64,256]{1,0:T(8,128)}), f32[64,256]{1,0:T(8,128)}) %all-reduce.13.cloned.1.call-update) | async-done | bytes 65552
  189.7 0.7 constant_dynamic-slice_fusion
  190.5 0.1 maximum_bitcast_fusion
  190.6 0.7 fusion.45
  191.3 33.4 %all_gather.16 = bf16[4,8192]{1,0:T(4,128)(2,1)S(1)} all-gather(bf16[4,256]{1,0:T(4,128)(2,1)S(1)} %fusion.45), channel_id=1, replica_groups=mesh['gx'=16,'gy'=32] {'gy'}, dimensions={1}, use_global_device_ids=true | all-gather | bytes 67584 | tf_op jit(solution)/shard_map/all_gather | solution.py:85
  224.8 0.1 fusion.66
  225.0 1.5 fusion.64
  226.5 87.9 %psum.51 = f32[4,8,6]{2,1,0:T(8,128)S(1)} all-reduce(f32[4,8,6]{2,1,0:T(8,128)S(1)} %get-tuple-element.21), channel_id=1, replica_groups=mesh['gx'=16,'gy'=32] {'gy'}, use_global_device_ids=true, to_apply=%region_5.6 | all-reduce | flops 192 | bytes 1536 | tf_op jit(solution)/shard_map/psum | solution.py:122
  314.4 0.9 fusion.12
  315.4 194.7 %all-reduce.9.cloned.1.call-done = f32[4,8,6,128]{3,2,1,0:T(8,128)} async-done(((f32[4,8,6,128]{3,2,1,0:T(8,128)}), f32[4,8,6,128]{3,2,1,0:T(8,128)}) %all-reduce.9.cloned.1.call-update) | async-done | bytes 98320 | tf_op jit(solution)/shard_map/psum | solution.py:122
  510.2 1.0 divide_convert_fusion
  511.2 0.1 dynamic-slice_bitcast_fusion
  511.3 17.9 %all-gather.1 = bf16[16,4,192]{2,1,0:T(4,128)(2,1)S(1)} all-gather(bf16[1,4,192]{2,1,0:T(4,128)(2,1)S(1)} %dynamic-slice_bitcast_fusion), channel_id=1, replica_groups=mesh['gx'=16,'gy'=32] {'gx'}, dimensions={0}, use_global_device_ids=true | all-gather | bytes 26112 | tf_op jit(solution)/shard_map/all_gather | solution.py:143
  529.3 0.8 fusion.67
  530.2 0.1 compare_reduce_fusion
  530.2 1.3 dynamic-slice.2
  532.2 186.1 %all-reduce.15.cloned.1.call-done = f32[64,384]{1,0:T(8,128)} async-done(((f32[64,384]{1,0:T(8,128)}), f32[64,384]{1,0:T(8,128)}) %all-reduce.15.cloned.1.call-update) | async-done | bytes 98320
  718.3 0.8 multiply_reduce_fusion.1
  719.2 33.1 %psum.52 = f32[2]{0:T(128)S(1)} all-reduce(f32[2]{0:T(128)S(1)} %multiply_reduce_fusion.1), channel_id=1, replica_groups=mesh['gx'=16,'gy'=32] {'gx'}, use_global_device_ids=true, to_apply=%region_8.9 | all-reduce | flops 2 | bytes 16 | tf_op jit(solution)/shard_map/psum | solution.py:150
  752.3 0.9 multiply_reduce_fusion
  753.2 0.1 fusion.49
  753.3 28.8 %all-reduce.3 = (f32[2]{0:T(128)S(1)}, f32[2,8]{1,0:T(2,128)S(1)}) all-reduce(f32[2]{0:T(128)S(1)} %get-tuple-element.4, f32[2,8]{1,0:T(2,128)S(1)} %fusion.49), channel_id=1, replica_groups=mesh['gx'=16,'gy'=32] {'gx'}, use_global_device_ids=true, to_apply=%region_10.11 | all-reduce | flops 18 | bytes 144 | tf_op jit(solution)/shard_map/psum | solution.py:153
  782.2 0.6 fusion.56
  782.8 0.2 fusion.58
  782.9 40.9 %all-gather.2 = bf16[32,2,384]{2,1,0:T(2,128)(2,1)S(1)} all-gather(bf16[1,2,384]{2,1,0:T(2,128)(2,1)S(1)} %get-tuple-element.12), channel_id=1, replica_groups=mesh['gx'=16,'gy'=32] {'gy'}, dimensions={0}, use_global_device_ids=true | all-gather | bytes 50688 | tf_op jit(solution)/shard_map/all_gather | solution.py:168
  823.9 1.2 fusion.2
  825.2 28.3 %all-gather.3 = bf16[32,2,2]{2,1,0:T(2,128)(2,1)S(1)} all-gather(bf16[1,2,2]{2,1,0:T(2,128)(2,1)S(1)} %fusion.59), channel_id=1, replica_groups=mesh['gx'=16,'gy'=32] {'gy'}, dimensions={0}, use_global_device_ids=true | all-gather | bytes 264 | tf_op jit(solution)/shard_map/all_gather | solution.py:169
  853.5 0.1 copy.58
  853.6 0.1 copy.59
  853.7 0.1 reshape.174
  853.8 76.7 %all-reduce.11.cloned.1.call-done = f32[32,2,2,512]{3,0,2,1:T(8,128)} async-done(((f32[32,2,2,512]{3,0,2,1:T(8,128)}), f32[32,2,2,512]{3,0,2,1:T(8,128)}) %all-reduce.11.cloned.1.call-update) | async-done | bytes 262160 | tf_op jit(solution)/shard_map/psum | solution.py:181
  930.5 1.2 convolution_bitcast_fusion.1
  931.7 0.3 fusion.6
  932.0 90.7 %all-reduce.2 = bf16[64,384]{1,0:T(8,128)(2,1)S(1)} all-reduce(f32[64,384]{1,0:T(8,128)S(1)} %fusion.6), channel_id=4, replica_groups=mesh['gx'=16,'gy'=32] {'gy'}, use_global_device_ids=true, to_apply=%region_18.19.clone | all-reduce | flops 24576 | bytes 147456
  1022.7 0.6 dynamic-slice_convert_fusion
  (49 shorter events, 1.0 us)
Async XLA Ops:
  7.2 816.8 %copy-start = (bf16[2,384,2,512]{3,2,1,0:T(2,128)(2,1)S(1)}, bf16[2,384,2,512]{3,2,1,0:T(2,128)(2,1)}, u32[]{:S(2)}) copy-start(bf16[2,384,2,512]{3,2,1,0:T(2,128)(2,1)} %param.26) | copy-start | bytes 4718596
  7.2 307.3 %copy-start.2 = (bf16[4,64,1024]{2,1,0:T(8,128)(2,1)S(1)}, bf16[4,64,1024]{2,1,0:T(8,128)(2,1)}, u32[]{:S(2)}) copy-start(bf16[4,64,1024]{2,1,0:T(8,128)(2,1)} %param.18) | copy-start | bytes 1572868
  7.2 182.5 %all-reduce.13.cloned.1.call-start = ((), (), s32[]{:S(2)}) async-start(), calls=%async_computation.2 | async-start | bytes 131072
  89.0 440.3 %copy-start.3 = (bf16[192,384]{1,0:T(8,128)(2,1)S(1)}, bf16[192,384]{1,0:T(8,128)(2,1)}, u32[]{:S(2)}) copy-start(bf16[192,384]{1,0:T(8,128)(2,1)} %param.21) | copy-start | bytes 442372
  89.1 421.1 %all-reduce.9.cloned.1.call-start = ((), (), s32[]{:S(2)}) async-start(), calls=%async_computation | async-start | bytes 262144 | tf_op jit(solution)/shard_map/psum | solution.py:122
  191.3 561.0 %copy-start.4 = (bf16[2,384]{1,0:T(2,128)(2,1)S(1)}, bf16[2,384]{1,0:T(2,128)(2,1)}, u32[]{:S(2)}) copy-start(bf16[2,384]{1,0:T(2,128)(2,1)} %param.14) | copy-start | bytes 4612
  191.3 561.0 %copy-start.6 = (f32[384]{0:T(512)S(1)}, f32[384]{0:T(512)}, u32[]{:S(2)}) copy-start(f32[384]{0:T(512)} %param.22) | copy-start | bytes 4612
  191.3 561.9 %copy-start.5 = (f32[384]{0:T(512)S(1)}, f32[384]{0:T(512)}, u32[]{:S(2)}) copy-start(f32[384]{0:T(512)} %param.23) | copy-start | bytes 4612
  191.3 561.9 %copy-start.7 = (bf16[384,8]{0,1:T(8,128)(2,1)S(1)}, bf16[384,8]{0,1:T(8,128)(2,1)}, u32[]{:S(2)}) copy-start(bf16[384,8]{0,1:T(8,128)(2,1)} %param.24) | copy-start | bytes 18436
  315.4 402.9 %all-reduce.15.cloned.1.call-start = ((), (), s32[]{:S(2)}) async-start(), calls=%async_computation.3 | async-start | bytes 196608
  511.2 419.3 %copy-start.1 = (bf16[2,512,384]{2,1,0:T(8,128)(2,1)S(1)}, bf16[2,512,384]{2,1,0:T(8,128)(2,1)}, u32[]{:S(2)}) copy-start(bf16[2,512,384]{2,1,0:T(8,128)(2,1)} %param.27) | copy-start | bytes 2359300
  530.1 400.4 %all-reduce.11.cloned.1.call-start = ((), (), s32[]{:S(2)}) async-start(), calls=%async_computation.1 | async-start | bytes 524288 | tf_op jit(solution)/shard_map/psum | solution.py:181
Sparse Core Ops, SparseCore 0:
  89.2 100.4 all-reduce.12
  315.5 194.6 all-reduce.8
  530.2 188.0 all-reduce.14
  825.3 105.1 all-reduce.10
where the time goes:
time: 1030 us
  waiting for transfers between devices  553 us (54%)
  blocking collectives  439 us (43%)
  between operations  15.3 us (1%)
    unnamed x6, waiting for transfers between devices  282 us
    psum x1, waiting for transfers between devices, local(): lax.psum((weighted_value_sum, denominator), 'gy')  195 us
    unnamed x1, blocking collectives  90.7 us
    psum x1, blocking collectives, local(): lax.psum((weighted_value_sum, denominator), 'gy')  87.9 us
    psum x1, waiting for transfers between devices, local(): lax.psum(jnp.einsum('qex,exuf->qeuf', slab_rows, w_gate_up, preferred_ele...  76.7 us
    all_gather x1, blocking collectives, local(): normed_all = lax.all_gather(normed, 'gy', axis=0, tiled=True)  44.1 us
    all_gather x1, blocking collectives, local(): lax.all_gather(moe_input, 'gy', axis=0, tiled=True)  40.9 us
    psum x1, blocking collectives, input_scale(): squares = lax.psum(jnp.sum(values * values, axis=-1), 'gx')  34.2 us
  transfers between devices with their start and end apart: 4, of which 4 were waited for; matrix products, arithmetic and copies ran while one was open for 1% of the time, Pallas kernels for 0%

commit v1 on v0

v1 whole, which is shorter than its diff:
```python
import functools
import math

import jax
import jax.numpy as jnp
from jax import lax
from jax.experimental import pallas as pl
from jax.experimental.pallas import tpu as pltpu
from jax.sharding import PartitionSpec as P

MODEL_WIDTH = 6144
QUERY_HEADS = 48
KEY_VALUE_HEADS = 8
HEAD_SIZE = 128
WINDOW_SLOTS = 2048
EXP_WIN = 2
NX, NY = 16, 32
EPS = 1e-05
CAP = 30.0
F32, BF16, I32 = jnp.float32, jnp.bfloat16, jnp.int32
MESH = pl.DeviceIdType.MESH

ST_B, ST_C, ST_D, ST_E, ST_F, ST_G, ST_J, ST_A, ST_K, ST_H, ST_L = range(11)


def iota(shape, dim):
    return lax.broadcasted_iota(I32, shape, dim)


def onehot(condition):
    return jnp.where(condition, 1.0, 0.0).astype(BF16)


def mm(a, b):
    return jnp.dot(a, b, preferred_element_type=F32)


def pick(number, values):
    result = values[-1]
    for k in range(len(values) - 2, -1, -1):
        result = jnp.where(number == k, values[k], result)
    return result


def gain_tile(row):
    s = iota((8, 128), 0)
    parts = [jnp.broadcast_to(row[:, 128 * c : 128 * c + 128], (8, 128)) for c in range(3)]
    return pick(s >> 1, parts + [jnp.ones((8, 128), F32)])


def fold_requests(v):
    u = v + pltpu.roll(v, 4, 0)
    return u + pltpu.roll(u, 2, 0)


def split_terms(v):
    hi = v.astype(BF16).astype(F32)
    rest = v - hi
    mid = rest.astype(BF16).astype(F32)
    low = rest - mid
    return hi + pltpu.roll(mid, 16, 1) + pltpu.roll(low, 32, 1)


def join_terms(v):
    return v + pltpu.roll(v, 112, 1) + pltpu.roll(v, 96, 1)


def as_rows(tile):
    return jnp.concatenate([tile[0:2], tile[2:4], tile[4:6]], axis=1)


def kernel(
    residual, attn_gain, wqkv, keys, values, lengths, starts, wo, post_gain, moe_gain, router, ids, w_gate_up, w_down,
    mixed_ref, out_ref,
    v_res, v_ag, v_pg, v_mg, v_rt, v_ids, v_wqkv, v_keys, v_vals, v_wo, v_gu, v_wd, w_split,
    perm_c, sel_e, sel_g, perm_k, perm_l, rm, mask, base_t, branch_t, q_rows, x_moe,
    t_b, r_b, s_c, r_c, t_d, r_d, s_e, r_e, t_f, r_f, s_g, r_g, t_j, r_j, s_a, r_a, s_k, r_k, t_h, r_h, s_l, r_l,
    load_sem, send_sem, recv_sem,
):
    gx = lax.axis_index("gx")
    gy = lax.axis_index("gy")
    z, core = lax.div(gy, 2), lax.rem(gy, 2)
    px, py = lax.div(gx, 4), lax.rem(gx, 4)

    loads = []

    def load(src, dst, k):
        c = pltpu.make_async_copy(src, dst, load_sem.at[k])
        c.start()
        loads.append(c)

    load(residual, v_res, 0)
    load(attn_gain, v_ag, 1)
    load(post_gain, v_pg, 2)
    load(moe_gain, v_mg, 3)
    load(router, v_rt, 4)
    load(ids, v_ids, 5)
    load(wqkv, v_wqkv, 6)
    load(keys, v_keys, 7)
    load(values, v_vals, 8)
    load(wo.at[pl.ds(pl.multiple_of(64 * core, 64), 128)], v_wo.at[pl.ds(0, 128)], 9)
    load(
        wo.at[pl.ds(pl.multiple_of(128 * (1 - core), 64), 64)],
        v_wo.at[pl.ds(pl.multiple_of(128 + 64 * core, 64), 64)],
        10,
    )
    load(w_gate_up, v_gu, 11)
    load(w_down, v_wd, 12)

    def over_gy(act):
        def body(q, carry):
            h = lax.div(q + 1, 2)
            far = lax.rem(z + 8 + h * (1 - 2 * lax.rem(q, 2)), 16)
            act(2 * far + core)
            act(2 * far + 1 - core)
            return carry

        lax.fori_loop(0, 15, body, 0)
        act(2 * z + 1 - core)

    def over_gx(act):
        def shift(t):
            return lax.rem(10 - lax.div(t * (t + 1), 2), 4)

        def body(k, carry):
            qx = lax.rem(px + shift(lax.div(k, 4)), 4)
            qy = lax.rem(py + shift(lax.rem(k, 4)), 4)
            act(4 * qx + qy)
            return carry

        lax.fori_loop(0, 15, body, 0)

    barrier = pltpu.get_barrier_semaphore()
    over_gy(lambda p: pl.semaphore_signal(barrier, inc=1, device_id=(gx, p), device_id_type=MESH))
    over_gx(lambda p: pl.semaphore_signal(barrier, inc=1, device_id=(p, gy), device_id_type=MESH))

    def send(stage, along, src, dst, each):
        me = gy if along == "gy" else gx

        def act(p):
            pltpu.make_async_remote_copy(
                src_ref=src.at[p] if each else src,
                dst_ref=dst.at[me],
                send_sem=send_sem.at[stage],
                recv_sem=recv_sem.at[stage],
                device_id=(gx, p) if along == "gy" else (p, gy),
                device_id_type=MESH,
            ).start()

        (over_gy if along == "gy" else over_gx)(act)
        dst[me] = src[me] if each else src[...]

    def peers_of(dst):
        return dst.at[pl.ds(0, dst.shape[0] - 1)]

    def received(stage, dst):
        pltpu.make_async_copy(peers_of(dst), peers_of(dst), recv_sem.at[stage]).wait()

    def total(ref):
        return jnp.sum(ref[...].astype(F32), axis=0)

    s8, l8 = iota((8, 128), 0), iota((8, 128), 1)
    for c in loads[:6]:
        c.wait()
    res = v_res[...].astype(F32)
    base = jnp.concatenate([res[:, 0:128], res[:, 128:256], res[:, 256:384], jnp.zeros((2, 128), F32)], axis=0)
    base_t[...] = base
    ag, pg, mg = gain_tile(v_ag[...]), gain_tile(v_pg[...]), gain_tile(v_mg[...])
    rt = v_rt[...].astype(F32)
    for e in range(8):
        row = rt[e : e + 1]
        parts = [jnp.broadcast_to(row[:, 128 * c : 128 * c + 128], (8, 128)) for c in range(3)]
        rm[e] = pick(s8 >> 1, parts + [jnp.zeros((8, 128), F32)]) * mg

    def lane_sums(terms):
        acc = jnp.zeros((8, 128), F32)
        for k, term in terms:
            acc = jnp.where(l8 == k, jnp.sum(term, axis=1, keepdims=True), acc)
        return fold_requests(acc)

    base_sums = lane_sums([(0, base * base)] + [(3 + e, base * rm[e]) for e in range(8)])
    t_b[...] = jnp.where(s8 < 6, base, split_terms(base_sums)).astype(BF16)

    row, lane = iota((512, 256), 0), iota((512, 256), 1)
    n = 4 * ((row >> 3) & 15) + (row & 3)
    perm_c[...] = onehot(lane == ((n >> 1) << 3) + 2 * (row >> 7) + (n & 1))

    pl.semaphore_wait(barrier, NX + NY - 2)
    send(ST_B, "gy", t_b, r_b, False)

    row, lane = iota((256, 256), 0), iota((256, 256), 1)
    j, t = row >> 3, (row >> 2) & 1
    head = 3 * (j >> 1) + jnp.where(t == 1, 1, 2 * (j & 1))
    sel_e[...] = onehot(lane == ((head >> 1) << 3) + ((head & 1) << 2) + (row & 3))

    row, lane = iota((512, 128), 0), iota((512, 128), 1)
    s = row & 7
    n = 2 * ((row >> 3) & 31) + (s & 1)
    sel_g[...] = onehot((lane == ((n >> 2) << 3) + ((row >> 8) << 2) + (n & 3)) & (s < 6))

    lane_code, row_code = [], []
    id_rows = v_ids[...]
    for e in range(EXP_WIN):
        picked = jnp.where((id_rows[0:1] == e) | (id_rows[1:2] == e), 1.0, 0.0)
        a, b = iota((64, 64), 0), iota((64, 64), 1)
        column = jnp.sum(jnp.where(a == b, picked, 0.0), axis=1, keepdims=True)
        a, b = iota((64, 256), 0), iota((64, 256), 1)
        of = 2 * (b >> 3) + (b & 1)
        before = jnp.sum(jnp.where(a < of, column, 0.0), axis=0, keepdims=True)
        named = jnp.sum(jnp.where(a == of, column, 0.0), axis=0, keepdims=True)
        lane_code.append(jnp.where(named > 0.5, before, -1.0))
        a, b = iota((256, 64), 0), iota((256, 64), 1)
        of = 2 * (a >> 3) + (a & 1)
        before = jnp.sum(jnp.where(b < of, picked, 0.0), axis=1, keepdims=True)
        named = jnp.sum(jnp.where(b == of, picked, 0.0), axis=1, keepdims=True)
        row_code.append(jnp.where(named > 0.5, before, -1.0))

    row, lane = iota((128, 256), 0), iota((128, 256), 1)
    q, s = row & 7, lane & 7
    slot = (2 * (row >> 3) + (row & 1)).astype(F32)
    for e in range(EXP_WIN):
        here = slot == lane_code[e]
        for c in range(3):
            perm_k[pl.ds((3 * e + c) * 128, 128)] = onehot(here & ((s >> 1) == c))
    sums_here = (
        ((q >> 1) == 0) & (slot == lane_code[0]) | ((q >> 1) == 1) & (slot == lane_code[1])
    ) & ((s >> 1) == 3)
    own = ((q >> 1) == 2) & (lane == 8 * gy + 6 + (q & 1))
    perm_k[pl.ds(768, 128)] = onehot(sums_here | own)

    row, lane = iota((256, 256), 0), iota((256, 256), 1)
    slot = (2 * (lane >> 4) + (lane & 1)).astype(F32)
    for e in range(EXP_WIN):
        here = (slot == row_code[e]) & (((lane >> 3) & 1) == e) & ((row & 7) < 6)
        for ct in range(4):
            perm_l[pl.ds((4 * e + ct) * 256, 256)] = onehot(here & (((lane >> 1) & 3) == ct))

    row, lane = iota((8, 256), 0), iota((8, 256), 1)
    last = pick(lane >> 6, [lengths[r] for r in range(4)]) - 1
    first = pick(lane >> 6, [starts[r] for r in range(4)])
    position = last - ((last - (64 * gy + (lane & 63))) & (WINDOW_SLOTS - 1))
    usable = (position >= jnp.maximum(first, last - (WINDOW_SLOTS - 2))) & ((lane >> 6) == (row & 3))
    mask[...] = jnp.where(usable, 1.0, 0.0)

    turn = (l8 & 63).astype(F32)
    angle = pick(s8 & 3, [lengths[r] for r in range(4)]).astype(F32) * jnp.exp(turn * (-2.0 * math.log(10000.0) / 128))
    rotated = 2 * gy < QUERY_HEADS + KEY_VALUE_HEADS
    cosine = jnp.where(rotated, jnp.cos(angle), 1.0)
    sine = jnp.where(rotated, jnp.where(l8 < 64, -1.0, 1.0) * jnp.sin(angle), 0.0)

    v_wo[pl.ds(pl.multiple_of(192 - 64 * core, 64), 64)] = jnp.zeros((64, 384), BF16)
    loads[6].wait()

    received(ST_B, r_b)
    x = r_b[...].astype(F32)
    rows = mm(perm_c[...], (x * ag).reshape(256, 128).astype(BF16))
    left = jnp.concatenate([rows[128 * c : 128 * c + 128] for c in range(3)], axis=1).astype(BF16)
    sums = mm(left, v_wqkv[...])
    hh = (iota((128, 128), 0) >> 2) & 1
    sums = jnp.where(hh == 0, sums[:, 0:128], sums[:, 128:256])
    s_c[...] = jnp.concatenate([sums.reshape(16, 8, 128), rows[384:512].reshape(16, 8, 128)], axis=1).astype(BF16)
    send(ST_C, "gx", s_c, r_c, True)
    x_moe[...] = (x * mg).reshape(256, 128).astype(BF16)
    for c in loads[11:12]:
        c.wait()
    for e in range(EXP_WIN):
        for u in range(2):
            w_split[e, u] = v_gu[e, :, u, :]

    received(ST_C, r_c)
    both = total(r_c)
    square = join_terms(both[8:16])
    scale = lax.rsqrt(square[:, 0:1] / MODEL_WIDTH + EPS)
    heads = both[0:8] * scale
    heads = heads * cosine + pltpu.roll(heads, 64, 1) * sine
    t_d[...] = heads.astype(BF16)
    send(ST_D, "gy", t_d, r_d, False)

    def gate_up(x_rows, out):
        rows = mm(perm_k[...], x_rows)
        rows16 = rows.astype(BF16)
        ct = (iota((128, 128), 0) & 7) >> 1
        for e in range(EXP_WIN):
            left = jnp.concatenate([rows16[(3 * e + c) * 128 : (3 * e + c) * 128 + 128] for c in range(3)], axis=1)
            halves = []
            for u in range(2):
                full = mm(left, w_split[e, u])
                halves.append(pick(ct, [full[:, 128 * k : 128 * k + 128] for k in range(4)]).reshape(16, 8, 128))
            out[:, pl.ds(16 * e, 16), :] = jnp.concatenate(halves, axis=1).astype(BF16)
        sums = rows[768:896].reshape(16, 8, 128)
        out[:, pl.ds(32, 16), :] = jnp.concatenate([sums, jnp.zeros((16, 8, 128), F32)], axis=1).astype(BF16)

    gate_up(x_moe[...], s_a)
    send(ST_A, "gx", s_a, r_a, True)
    for c in loads[7:11] + loads[12:13]:
        c.wait()

    received(ST_D, r_d)
    everything = r_d[...].astype(F32).reshape(256, 128).astype(BF16)
    queries = mm(sel_e[...], everything)
    q_rows[...] = queries.reshape(32, 8, 128)
    queries = queries.astype(BF16)
    scores = []
    for g in range(KEY_VALUE_HEADS):
        kg = v_keys[:, :, pl.ds(128 * g, 128)].reshape(256, 128)
        scores.append(
            lax.dot_general(
                queries[32 * g : 32 * g + 32], kg, (((1,), (1,)), ((), ())), preferred_element_type=F32
            )
        )
    score = jnp.concatenate(scores, axis=0)
    weight = jnp.exp(CAP * jnp.tanh(score * (HEAD_SIZE**-0.5 / CAP))).reshape(32, 8, 256) * mask[...]
    weight = weight.reshape(256, 256)
    weight16 = weight.astype(BF16)
    sums = []
    for g in range(KEY_VALUE_HEADS):
        vg = v_vals[:, :, pl.ds(128 * g, 128)].reshape(256, 128)
        sums.append(mm(weight16[32 * g : 32 * g + 32], vg))
    summed = jnp.concatenate(sums, axis=0)
    total1 = jnp.broadcast_to(jnp.sum(weight, axis=1, keepdims=True), (256, 128))
    total0 = pltpu.roll(total1, 4, 0)
    row, lane = iota((256, 128), 0), iota((256, 128), 1)
    low1 = total1 - total1.astype(BF16).astype(F32)
    low0 = total0 - total0.astype(BF16).astype(F32)
    free = pick((lane & 63) >> 4, [total1, low1, total0, low0])
    keep = (((row >> 2) & 1) == 0) | ((lane >> 6) == ((row >> 3) & 1))
    s_e[...] = jnp.where(keep, summed, free).reshape(32, 8, 128).astype(BF16)
    send(ST_E, "gy", s_e, r_e, True)

    group = lax.div(gy, 4)
    second = lax.rem(group, 2)

    def fresh(first_block):
        tile = r_d[first_block + lax.div(group, 2)].astype(F32)
        return jnp.where((s8 >> 2) == second, tile, pltpu.roll(tile, 4, 0))

    own_query = q_rows[gy].astype(BF16).astype(F32)
    own_score = jnp.sum(own_query * fresh(24), axis=1, keepdims=True) * (HEAD_SIZE**-0.5 / CAP)
    own_weight = jnp.exp(CAP * jnp.tanh(own_score))
    own_value = own_weight.astype(BF16).astype(F32) * fresh(28)
    total_a = None

    received(ST_E, r_e)
    tile = total(r_e)
    half = (l8 >> 6) == core
    quarter = (l8 & 63) >> 5
    den1 = jnp.sum(jnp.where(~half & (quarter == 0), tile, 0.0), axis=1, keepdims=True) * 0.0625
    den0 = jnp.sum(jnp.where(~half & (quarter == 1), tile, 0.0), axis=1, keepdims=True) * 0.0625
    den1, den0 = jnp.broadcast_to(den1, (8, 128)), jnp.broadcast_to(den0, (8, 128))
    den = jnp.where(s8 < 4, pltpu.roll(den0, 4, 0), den1) + own_weight
    attended = (tile + own_value) / den
    t_f[...] = jnp.where((s8 < 4) | half, attended, 0.0).astype(BF16)
    send(ST_F, "gx", t_f, r_f, False)

    ctile = (iota((256, 128), 0) & 7) >> 1
    received(ST_F, r_f)
    rows = mm(sel_g[...], r_f[...].astype(F32).reshape(128, 128).astype(BF16))
    left = jnp.concatenate([rows[0:256], rows[256:512]], axis=1).astype(BF16)
    sums = mm(left, v_wo[...])
    s_g[...] = pick(ctile, [sums[:, 128 * c : 128 * c + 128] for c in range(3)]).reshape(32, 8, 128).astype(BF16)
    send(ST_G, "gy", s_g, r_g, True)
    received(ST_A, r_a)
    total_a = total(r_a)

    received(ST_G, r_g)
    branch = jnp.where(s8 < 6, total(r_g), 0.0)
    gained = branch * pg
    branch_t[...] = gained
    branch_sums = lane_sums(
        [(0, branch * branch), (1, base_t[...] * gained), (2, gained * gained)]
        + [(3 + e, gained * rm[e]) for e in range(8)]
    )
    t_j[...] = jnp.where(s8 < 6, gained * mg, split_terms(branch_sums)).astype(BF16)
    send(ST_J, "gy", t_j, r_j, False)

    received(ST_J, r_j)
    gate_up(r_j[...].astype(F32).reshape(256, 128).astype(BF16), s_k)
    send(ST_K, "gx", s_k, r_k, True)
    received(ST_K, r_k)
    total_k = total(r_k)

    sums_a, sums_k = join_terms(total_a[32:40]), join_terms(total_k[32:40])
    post = lax.rsqrt(sums_k[:, 0:1] / MODEL_WIDTH + EPS)
    stream_square = sums_a[:, 0:1] + 2.0 * post * sums_k[:, 1:2] + post * post * sums_k[:, 2:3]
    pre = lax.rsqrt(stream_square / MODEL_WIDTH + EPS)
    logits = pre * (sums_a + post * sums_k)
    named = (l8 >= 3) & (l8 < 11)
    exponent = jnp.where(named, jnp.exp(jnp.where(named, logits, 0.0)), 0.0)
    chance = exponent / jnp.sum(exponent, axis=1, keepdims=True)
    combine = jnp.sum(jnp.where(l8 == 3 + (s8 >> 1), chance, 0.0), axis=1, keepdims=True)
    combine = combine.astype(BF16).astype(F32)

    def spread(column, first):
        two = [jnp.broadcast_to(column[first + k : first + k + 1], (8, 128)) for k in range(2)]
        return jnp.where((s8 & 1) == 0, two[0], two[1])

    hidden = []
    for e in range(EXP_WIN):
        post_e, pre_e = spread(post, 2 * e), spread(pre, 2 * e)
        gate, up = (
            pre_e * (total_a[16 * e + 8 * u : 16 * e + 8 * u + 8] + post_e * total_k[16 * e + 8 * u : 16 * e + 8 * u + 8])
            for u in range(2)
        )
        bent = 0.5 * gate * (1.0 + jnp.tanh(math.sqrt(2.0 / math.pi) * (gate + 0.044715 * gate * gate * gate)))
        hidden.append(bent * up * spread(combine, 2 * e))
    t_h[...] = jnp.concatenate(hidden, axis=0).astype(BF16)
    send(ST_H, "gx", t_h, r_h, False)

    mixed_ref[...] = as_rows(base_t[...] + spread(post, 4) * branch_t[...]).astype(BF16)

    received(ST_H, r_h)
    hidden = r_h[...].astype(F32).reshape(256, 128).astype(BF16)
    sums = jnp.zeros((256, 384), F32)
    for e in range(EXP_WIN):
        rows = mm(perm_l[pl.ds(1024 * e, 1024)], hidden).astype(BF16)
        left = jnp.concatenate([rows[256 * ct : 256 * ct + 256] for ct in range(4)], axis=1)
        sums = sums + mm(left, v_wd[e])
    s_l[...] = pick(ctile, [sums[:, 128 * c : 128 * c + 128] for c in range(3)]).reshape(32, 8, 128).astype(BF16)
    send(ST_L, "gy", s_l, r_l, True)
    received(ST_L, r_l)
    out_ref[...] = as_rows(total(r_l)).astype(BF16)

    for stage, dst in (
        (ST_B, r_b), (ST_C, r_c), (ST_D, r_d), (ST_E, r_e), (ST_F, r_f), (ST_G, r_g), (ST_J, r_j), (ST_A, r_a),
        (ST_K, r_k), (ST_H, r_h), (ST_L, r_l),
    ):
        pltpu.make_async_copy(peers_of(dst), peers_of(dst), send_sem.at[stage]).wait()


def local(
    residual, attn_gain, wqkv, rotated_key_cache, slot_value_cache, lengths, starts, wo, post_gain, moe_gain, router,
    expert_ids, w_gate_up, w_down,
):
    anywhere = pl.BlockSpec(memory_space=pl.ANY)
    scalars = pl.BlockSpec(memory_space=pltpu.SMEM)
    vmem = pltpu.VMEM
    gy_tiles = vmem((NY, 8, 128), BF16)
    gx_tiles = vmem((NX, 8, 128), BF16)
    tile = vmem((8, 128), BF16)
    return pl.pallas_call(
        kernel,
        out_shape=(jax.ShapeDtypeStruct((2, 384), BF16), jax.ShapeDtypeStruct((2, 384), BF16)),
        in_specs=[anywhere] * 5 + [scalars] * 2 + [anywhere] * 7,
        out_specs=(pl.BlockSpec(memory_space=pltpu.VMEM), pl.BlockSpec(memory_space=pltpu.VMEM)),
        scratch_shapes=[
            vmem((2, 384), BF16), vmem((1, 384), F32), vmem((1, 384), F32), vmem((1, 384), F32), vmem((8, 384), BF16),
            vmem((2, 64), I32), vmem((384, 256), BF16), vmem((4, 64, 1024), BF16), vmem((4, 64, 1024), BF16),
            vmem((256, 384), BF16), vmem((2, 384, 2, 512), BF16), vmem((2, 512, 384), BF16),
            vmem((2, 2, 384, 512), BF16),
            vmem((512, 256), BF16), vmem((256, 256), BF16), vmem((512, 128), BF16), vmem((896, 256), BF16),
            vmem((2048, 256), BF16), vmem((8, 8, 128), F32), vmem((8, 256), F32), vmem((8, 128), F32),
            vmem((8, 128), F32), vmem((32, 8, 128), F32), vmem((256, 128), BF16),
            tile, gy_tiles, vmem((NX, 16, 128), BF16), vmem((NX, 16, 128), BF16), tile, gy_tiles, gy_tiles, gy_tiles,
            tile, gx_tiles, gy_tiles, gy_tiles, tile, gy_tiles, vmem((NX, 48, 128), BF16), vmem((NX, 48, 128), BF16),
            vmem((NX, 48, 128), BF16), vmem((NX, 48, 128), BF16), vmem((16, 128), BF16), vmem((NX, 16, 128), BF16),
            gy_tiles, gy_tiles,
            pltpu.SemaphoreType.DMA((13,)), pltpu.SemaphoreType.DMA((11,)), pltpu.SemaphoreType.DMA((11,)),
        ],
        compiler_params=pltpu.CompilerParams(
            collective_id=0, has_side_effects=True, vmem_limit_bytes=48 * 1024 * 1024
        ),
        name="decode_step",
    )(
        residual, attn_gain.reshape(1, 384), wqkv, rotated_key_cache, slot_value_cache, lengths, starts, wo,
        post_gain.reshape(1, 384), moe_gain.reshape(1, 384), router.T, expert_ids.T, w_gate_up, w_down,
    )


def solution(mesh):
    return jax.shard_map(
        local,
        mesh=mesh,
        in_specs=(
            P("gy", "gx"), P("gx"), P("gx", "gy"), P("gx", "gy", None), P("gx", "gy", None), P("gx"), P("gx"),
            P("gy", "gx"), P("gx"), P("gx"), P("gx", None), P(), P(None, "gx", None, "gy"), P(None, "gy", "gx"),
        ),
        out_specs=(P("gy", "gx"), P("gy", "gx")),
        check_vma=False,
    )
```

time: 1030 us -> 98.7 us (0.10)
  waiting for transfers between devices: 553 us -> 0 us
  blocking collectives: 439 us -> 0 us
  Pallas kernels: 0 us -> 84.6 us
  between operations: 15.3 us -> 0.65 us
    unnamed x6 -> x0, waiting for transfers between devices: 282 us -> none
    psum x2 -> x0, waiting for transfers between devices: 271 us -> none  [the longest x1 195 us: local(): lax.psum((weighted_value_sum, denominator), 'gy')]
    psum x4 -> x0, blocking collectives: 184 us -> none  [the longest x1 87.9 us: local(): lax.psum((weighted_value_sum, denominator), 'gy')]
    all_gather x5 -> x0, blocking collectives: 165 us -> none  [the longest x1 44.1 us: local(): normed_all = lax.all_gather(normed, 'gy', axis=0, tiled=True)]
    unnamed x1 -> x0, blocking collectives: 90.7 us -> none
    pallas_call x0 -> x1, Pallas kernels: none -> 84.6 us  [local(): pl.pallas_call(kernel, out_shape=(jax.ShapeDtypeStruct((2, 384), BF16), j...]
  transfers between devices with their start and end apart: 4 -> 0, of which waited for: 4 -> 0; matrix products, arithmetic and copies ran while one was open for 1% -> 0% of each run, Pallas kernels for 0% -> 0%
where the time goes in v1:
time: 98.7 us; the launch traced here: 98.2 us
  Pallas kernels  84.6 us (86%)
  local copies, waits for them, and re-layouts  13 us (13%)
    pallas_call x1, Pallas kernels, local(): pl.pallas_call(kernel, out_shape=(jax.ShapeDtypeStruct((2, 384), BF16), j...  84.6 us
    unnamed x24, local copies, waits for them, and re-layouts  10.9 us

profile of v1, /device:TPU:1, one launch (start us, length us, event | category | flops | bytes accessed | tf_op | source)
XLA Modules:
  0.0 98.2 jit_solution(13551287559850356847)
XLA Ops:
  0.6 0.7 reshape.13.attn_gain
  1.3 0.7 reshape.14.post_gain
  2.0 0.7 reshape.15.moe_gain
  2.7 0.0 copy-start
  2.7 1.4 %copy-done = bf16[2,384,2,512]{3,2,1,0:T(2,128)(2,1)S(1)} copy-done((bf16[2,384,2,512]{3,2,1,0:T(2,128)(2,1)S(1)}, bf16[2,384,2,512]{3,2,1,0:T(2,128)(2,1)}, u32[]{:S(2)}) %copy-start) | copy-done | bytes 1572888
  4.1 0.0 copy-start.1
  4.1 1.1 %copy-done.1 = bf16[2,512,384]{2,1,0:T(8,128)(2,1)S(1)} copy-done((bf16[2,512,384]{2,1,0:T(8,128)(2,1)S(1)}, bf16[2,512,384]{2,1,0:T(8,128)(2,1)}, u32[]{:S(2)}) %copy-start.1) | copy-done | bytes 786456
  5.2 0.0 copy-start.2
  5.2 1.0 %copy-done.2 = bf16[4,64,1024]{2,1,0:T(8,128)(2,1)S(1)} copy-done((bf16[4,64,1024]{2,1,0:T(8,128)(2,1)S(1)}, bf16[4,64,1024]{2,1,0:T(8,128)(2,1)}, u32[]{:S(2)}) %copy-start.2) | copy-done | bytes 524312
  6.3 0.0 copy-start.3
  6.3 1.0 %copy-done.3 = bf16[4,64,1024]{2,1,0:T(8,128)(2,1)S(1)} copy-done((bf16[4,64,1024]{2,1,0:T(8,128)(2,1)S(1)}, bf16[4,64,1024]{2,1,0:T(8,128)(2,1)}, u32[]{:S(2)}) %copy-start.3) | copy-done | bytes 524312
  7.3 0.0 copy-start.4
  7.3 0.9 copy-done.4
  8.2 0.0 copy-start.5
  8.2 0.9 copy-done.5
  9.1 0.0 copy-start.6
  9.1 0.7 copy-done.6
  9.8 0.0 copy-start.7
  9.8 0.7 copy-done.7
  10.5 0.0 copy-start.8
  10.5 0.7 copy-done.8
  11.2 0.0 copy-start.9
  11.2 0.7 copy-done.9
  11.9 0.0 copy-start.10
  11.9 0.7 copy-done.10
  12.5 84.6 %decode_step.1 = (bf16[2,384]{1,0:T(2,128)(2,1)S(1)}, bf16[2,384]{1,0:T(2,128)(2,1)S(1)}) custom-call(bf16[2,384]{1,0:T(2,128)(2,1)S(1)} %copy-done.7, f32[1,384]{1,0:T(1,128)S(1)} %reshape.13.attn_gain, bf16[384,256]{1,0:T(8,128)(2,1)S(1)} %copy-done.4, bf16[4,64,1024]{2,1,0:T(8,128)(2,1)S(1)} %copy-done.2, bf16[4,64,1024]{2,1,0:T(8,128)(2,1)S(1)} %copy-done.3, ...), custom_call_target="tpu_custom_call" | custom-call | tf_op jit(solution)/shard_map/decode_step/pallas_call | solution.py:440
  97.1 0.6 copy.18
  97.7 0.6 copy.19
Async XLA Ops:
  2.7 1.4 %copy-start = (bf16[2,384,2,512]{3,2,1,0:T(2,128)(2,1)S(1)}, bf16[2,384,2,512]{3,2,1,0:T(2,128)(2,1)}, u32[]{:S(2)}) copy-start(bf16[2,384,2,512]{3,2,1,0:T(2,128)(2,1)} %w_gate_up.1) | copy-start | bytes 4718596
  4.1 1.1 %copy-start.1 = (bf16[2,512,384]{2,1,0:T(8,128)(2,1)S(1)}, bf16[2,512,384]{2,1,0:T(8,128)(2,1)}, u32[]{:S(2)}) copy-start(bf16[2,512,384]{2,1,0:T(8,128)(2,1)} %w_down.1) | copy-start | bytes 2359300
  5.2 1.0 %copy-start.2 = (bf16[4,64,1024]{2,1,0:T(8,128)(2,1)S(1)}, bf16[4,64,1024]{2,1,0:T(8,128)(2,1)}, u32[]{:S(2)}) copy-start(bf16[4,64,1024]{2,1,0:T(8,128)(2,1)} %keys.1) | copy-start | bytes 1572868
  6.3 1.0 %copy-start.3 = (bf16[4,64,1024]{2,1,0:T(8,128)(2,1)S(1)}, bf16[4,64,1024]{2,1,0:T(8,128)(2,1)}, u32[]{:S(2)}) copy-start(bf16[4,64,1024]{2,1,0:T(8,128)(2,1)} %values.1) | copy-start | bytes 1572868
  7.3 0.9 copy-start.4
  8.2 0.9 copy-start.5
  9.1 0.7 copy-start.6
  9.8 0.7 copy-start.7
  10.5 0.7 copy-start.8
  11.2 0.7 copy-start.9
  11.9 0.7 copy-start.10

commit v2 on v1

--- a/solution.py
+++ b/solution.py
@@ -42,9 +42,9 @@
     return result
 
 
-def gain_tile(row):
+def gain_tile(gain):
     s = iota((8, 128), 0)
-    parts = [jnp.broadcast_to(row[:, 128 * c : 128 * c + 128], (8, 128)) for c in range(3)]
+    parts = [jnp.broadcast_to(gain[pl.ds(128 * c, 128)].reshape(1, 128), (8, 128)) for c in range(3)]
     return pick(s >> 1, parts + [jnp.ones((8, 128), F32)])
 
 
@@ -71,7 +71,7 @@
 
 def kernel(
     residual, attn_gain, wqkv, keys, values, lengths, starts, wo, post_gain, moe_gain, router, ids, w_gate_up, w_down,
-    mixed_ref, out_ref,
+    res_ref,
     v_res, v_ag, v_pg, v_mg, v_rt, v_ids, v_wqkv, v_keys, v_vals, v_wo, v_gu, v_wd, w_split,
     perm_c, sel_e, sel_g, perm_k, perm_l, rm, mask, base_t, branch_t, q_rows, x_moe,
     t_b, r_b, s_c, r_c, t_d, r_d, s_e, r_e, t_f, r_f, s_g, r_g, t_j, r_j, s_a, r_a, s_k, r_k, t_h, r_h, s_l, r_l,
@@ -81,6 +81,33 @@
     gy = lax.axis_index("gy")
     z, core = lax.div(gy, 2), lax.rem(gy, 2)
     px, py = lax.div(gx, 4), lax.rem(gx, 4)
+
+    def over_gy(act):
+        def body(q, carry):
+            h = lax.div(q + 1, 2)
+            far = lax.rem(z + 8 + h * (1 - 2 * lax.rem(q, 2)), 16)
+            act(2 * far + core)
+            act(2 * far + 1 - core)
+            return carry
+
+        lax.fori_loop(0, 15, body, 0)
+        act(2 * z + 1 - core)
+
+    def over_gx(act):
+        def shift(t):
+            return lax.rem(10 - lax.div(t * (t + 1), 2), 4)
+
+        def body(k, carry):
+            qx = lax.rem(px + shift(lax.div(k, 4)), 4)
+            qy = lax.rem(py + shift(lax.rem(k, 4)), 4)
+            act(4 * qx + qy)
+            return carry
+
+        lax.fori_loop(0, 15, body, 0)
+
+    barrier = pltpu.get_barrier_semaphore()
+    over_gy(lambda p: pl.semaphore_signal(barrier, inc=1, device_id=(gx, p), device_id_type=MESH))
+    over_gx(lambda p: pl.semaphore_signal(barrier, inc=1, device_id=(p, gy), device_id_type=MESH))
 
     loads = []
 
@@ -107,33 +134,6 @@
     load(w_gate_up, v_gu, 11)
     load(w_down, v_wd, 12)
 
-    def over_gy(act):
-        def body(q, carry):
-            h = lax.div(q + 1, 2)
-            far = lax.rem(z + 8 + h * (1 - 2 * lax.rem(q, 2)), 16)
-            act(2 * far + core)
-            act(2 * far + 1 - core)
-            return carry
-
-        lax.fori_loop(0, 15, body, 0)
-        act(2 * z + 1 - core)
-
-    def over_gx(act):
-        def shift(t):
-            return lax.rem(10 - lax.div(t * (t + 1), 2), 4)
-
-        def body(k, carry):
-            qx = lax.rem(px + shift(lax.div(k, 4)), 4)
-            qy = lax.rem(py + shift(lax.rem(k, 4)), 4)
-            act(4 * qx + qy)
-            return carry
-
-        lax.fori_loop(0, 15, body, 0)
-
-    barrier = pltpu.get_barrier_semaphore()
-    over_gy(lambda p: pl.semaphore_signal(barrier, inc=1, device_id=(gx, p), device_id_type=MESH))
-    over_gx(lambda p: pl.semaphore_signal(barrier, inc=1, device_id=(p, gy), device_id_type=MESH))
-
     def send(stage, along, src, dst, each):
         me = gy if along == "gy" else gx
 
@@ -165,7 +165,7 @@
     res = v_res[...].astype(F32)
     base = jnp.concatenate([res[:, 0:128], res[:, 128:256], res[:, 256:384], jnp.zeros((2, 128), F32)], axis=0)
     base_t[...] = base
-    ag, pg, mg = gain_tile(v_ag[...]), gain_tile(v_pg[...]), gain_tile(v_mg[...])
+    ag, pg, mg = gain_tile(v_ag), gain_tile(v_pg), gain_tile(v_mg)
     rt = v_rt[...].astype(F32)
     for e in range(8):
         row = rt[e : e + 1]
@@ -406,7 +406,7 @@
     t_h[...] = jnp.concatenate(hidden, axis=0).astype(BF16)
     send(ST_H, "gx", t_h, r_h, False)
 
-    mixed_ref[...] = as_rows(base_t[...] + spread(post, 4) * branch_t[...]).astype(BF16)
+    mixed = as_rows(base_t[...] + spread(post, 4) * branch_t[...])
 
     received(ST_H, r_h)
     hidden = r_h[...].astype(F32).reshape(256, 128).astype(BF16)
@@ -418,7 +418,7 @@
     s_l[...] = pick(ctile, [sums[:, 128 * c : 128 * c + 128] for c in range(3)]).reshape(32, 8, 128).astype(BF16)
     send(ST_L, "gy", s_l, r_l, True)
     received(ST_L, r_l)
-    out_ref[...] = as_rows(total(r_l)).astype(BF16)
+    res_ref[...] = jnp.concatenate([mixed, as_rows(total(r_l))], axis=0).astype(BF16)
 
     for stage, dst in (
         (ST_B, r_b), (ST_C, r_c), (ST_D, r_d), (ST_E, r_e), (ST_F, r_f), (ST_G, r_g), (ST_J, r_j), (ST_A, r_a),
@@ -431,19 +431,19 @@
     residual, attn_gain, wqkv, rotated_key_cache, slot_value_cache, lengths, starts, wo, post_gain, moe_gain, router,
     expert_ids, w_gate_up, w_down,
 ):
-    anywhere = pl.BlockSpec(memory_space=pl.ANY)
+    anywhere = pl.BlockSpec(memory_space=pltpu.HBM)
     scalars = pl.BlockSpec(memory_space=pltpu.SMEM)
     vmem = pltpu.VMEM
     gy_tiles = vmem((NY, 8, 128), BF16)
     gx_tiles = vmem((NX, 8, 128), BF16)
     tile = vmem((8, 128), BF16)
-    return pl.pallas_call(
+    result = pl.pallas_call(
         kernel,
-        out_shape=(jax.ShapeDtypeStruct((2, 384), BF16), jax.ShapeDtypeStruct((2, 384), BF16)),
+        out_shape=jax.ShapeDtypeStruct((4, 384), BF16),
         in_specs=[anywhere] * 5 + [scalars] * 2 + [anywhere] * 7,
-        out_specs=(pl.BlockSpec(memory_space=pltpu.VMEM), pl.BlockSpec(memory_space=pltpu.VMEM)),
+        out_specs=pl.BlockSpec(memory_space=pltpu.VMEM),
         scratch_shapes=[
-            vmem((2, 384), BF16), vmem((1, 384), F32), vmem((1, 384), F32), vmem((1, 384), F32), vmem((8, 384), BF16),
+            vmem((2, 384), BF16), vmem((384,), F32), vmem((384,), F32), vmem((384,), F32), vmem((8, 384), BF16),
             vmem((2, 64), I32), vmem((384, 256), BF16), vmem((4, 64, 1024), BF16), vmem((4, 64, 1024), BF16),
             vmem((256, 384), BF16), vmem((2, 384, 2, 512), BF16), vmem((2, 512, 384), BF16),
             vmem((2, 2, 384, 512), BF16),
@@ -457,13 +457,14 @@
             pltpu.SemaphoreType.DMA((13,)), pltpu.SemaphoreType.DMA((11,)), pltpu.SemaphoreType.DMA((11,)),
         ],
         compiler_params=pltpu.CompilerParams(
-            collective_id=0, has_side_effects=True, vmem_limit_bytes=48 * 1024 * 1024
+            collective_id=0, has_side_effects=True, vmem_limit_bytes=63 * 1024 * 1024
         ),
         name="decode_step",
     )(
-        residual, attn_gain.reshape(1, 384), wqkv, rotated_key_cache, slot_value_cache, lengths, starts, wo,
-        post_gain.reshape(1, 384), moe_gain.reshape(1, 384), router.T, expert_ids.T, w_gate_up, w_down,
+        residual, attn_gain, wqkv, rotated_key_cache, slot_value_cache, lengths, starts, wo,
+        post_gain, moe_gain, router.T, expert_ids.T, w_gate_up, w_down,
     )
+    return result[:2], result[2:]
 
 
 def solution(mesh):

time: 98.7 us -> 86.9 us (0.88)
  local copies, waits for them, and re-layouts: 13 us -> 1.32 us
    unnamed x24 -> x0, local copies, waits for them, and re-layouts: 10.9 us -> none
    reshape x3 -> x0, local copies, waits for them, and re-layouts: 2.05 us -> none  [the longest x1 0.68 us: local(): attn_gain.reshape(1, 384)]
    slice x0 -> x1, local copies, waits for them, and re-layouts: none -> 1.32 us  [local(): return (result[:2], result[2:])]
where the time goes in v2:
time: 86.9 us; the launch traced here: 86.7 us
  Pallas kernels  84.7 us (97%)
  local copies, waits for them, and re-layouts  1.32 us (2%)
    pallas_call x1, Pallas kernels, local(): pl.pallas_call(kernel, out_shape=jax.ShapeDtypeStruct((4, 384), BF16), in...  84.7 us

profile of v2, /device:TPU:1, one launch (start us, length us, event | category | flops | bytes accessed | tf_op | source)
XLA Modules:
  0.0 86.7 jit_solution(18029140410042324381)
XLA Ops:
  0.6 84.7 %decode_step.1 = bf16[4,384]{1,0:T(4,128)(2,1)} custom-call(bf16[2,384]{1,0:T(2,128)(2,1)} %residual.1, f32[384]{0:T(512)} %attn_gain.1, bf16[384,256]{1,0:T(8,128)(2,1)} %wqkv.1, bf16[4,64,1024]{2,1,0:T(8,128)(2,1)} %keys.1, bf16[4,64,1024]{2,1,0:T(8,128)(2,1)} %values.1, s32[4]{0:T(128)} %lengths.1, s32[4]{0:T(128)} %starts.1, bf16[192,384]{1,0:T(8,128)(2,1)} %wo.1, ...), custom_call_target="tpu_custom_call" | custom-call | tf_op jit(solution)/shard_map/decode_step/pallas_call | solution.py:440
  85.4 1.3 %fusion = (bf16[2,384]{1,0:T(2,128)(2,1)}, bf16[2,384]{1,0:T(2,128)(2,1)}) fusion(bf16[4,384]{1,0:T(4,128)(2,1)} %decode_step.1), kind=kLoop, calls=%fused_computation | loop fusion | bytes 6144 | tf_op jit(solution)/shard_map/slice | solution.py:467

commit v3 on v2

--- a/solution.py
+++ b/solution.py
@@ -20,7 +20,7 @@
 F32, BF16, I32 = jnp.float32, jnp.bfloat16, jnp.int32
 MESH = pl.DeviceIdType.MESH
 
-ST_B, ST_C, ST_D, ST_E, ST_F, ST_G, ST_J, ST_A, ST_K, ST_H, ST_L = range(11)
+ST_B, ST_C, ST_D, ST_E, ST_F, ST_G, ST_J, ST_A, ST_K, ST_H, ST_L, ST_X = range(12)
 
 
 def iota(shape, dim):
@@ -65,6 +65,14 @@
     return v + pltpu.roll(v, 112, 1) + pltpu.roll(v, 96, 1)
 
 
+def place_of(n):
+    return (((n >> 2) & 7) << 2) + (((n >> 1) & 1) << 1) + (n >> 5)
+
+
+def request_at(index):
+    return (((index >> 5) + (((index >> 3) & 1) << 3)) << 2) + (((index >> 4) & 1) << 1) + (index & 1)
+
+
 def as_rows(tile):
     return jnp.concatenate([tile[0:2], tile[2:4], tile[4:6]], axis=1)
 
@@ -74,13 +82,16 @@
     res_ref,
     v_res, v_ag, v_pg, v_mg, v_rt, v_ids, v_wqkv, v_keys, v_vals, v_wo, v_gu, v_wd, w_split,
     perm_c, sel_e, sel_g, perm_k, perm_l, rm, mask, base_t, branch_t, q_rows, x_moe,
-    t_b, r_b, s_c, r_c, t_d, r_d, s_e, r_e, t_f, r_f, s_g, r_g, t_j, r_j, s_a, r_a, s_k, r_k, t_h, r_h, s_l, r_l,
+    t_b, r_b, s_c, r_c, t_d, r_d, s_e, r_e, t_f, r_f, s_x, r_x, s_g, r_g, t_j, r_j, s_a, r_a, s_k, r_k, t_h, r_h, s_l, r_l,
     load_sem, send_sem, recv_sem,
 ):
     gx = lax.axis_index("gx")
     gy = lax.axis_index("gy")
     z, core = lax.div(gy, 2), lax.rem(gy, 2)
     px, py = lax.div(gx, 4), lax.rem(gx, 4)
+    low_z, high = lax.rem(z, 8), lax.div(z, 8)
+    pair = 2 * low_z + core
+    place = 2 * pair + high
 
     def over_gy(act):
         def body(q, carry):
@@ -150,6 +161,35 @@
         (over_gy if along == "gy" else over_gx)(act)
         dst[me] = src[me] if each else src[...]
 
+    def over_z(act):
+        def body(q, carry):
+            h = lax.div(q + 1, 2)
+            act(lax.rem(z + 8 + h * (1 - 2 * lax.rem(q, 2)), 16))
+            return carry
+
+        lax.fori_loop(0, 15, body, 0)
+
+    def over_near(act):
+        def body(q, carry):
+            h = lax.div(q + 1, 2)
+            near = lax.rem(z + 16 + (4 - h) * (2 * lax.rem(q, 2) - 1), 16)
+            act(2 * near + core)
+            act(2 * near + 1 - core)
+            return carry
+
+        lax.fori_loop(0, 7, body, 0)
+        act(2 * z + 1 - core)
+
+    def push(stage, src, dst, p):
+        pltpu.make_async_remote_copy(
+            src_ref=src,
+            dst_ref=dst,
+            send_sem=send_sem.at[stage],
+            recv_sem=recv_sem.at[stage],
+            device_id=(gx, p),
+            device_id_type=MESH,
+        ).start()
+
     def peers_of(dst):
         return dst.at[pl.ds(0, dst.shape[0] - 1)]
 
@@ -183,10 +223,11 @@
 
     row, lane = iota((512, 256), 0), iota((512, 256), 1)
     n = 4 * ((row >> 3) & 15) + (row & 3)
-    perm_c[...] = onehot(lane == ((n >> 1) << 3) + 2 * (row >> 7) + (n & 1))
+    perm_c[...] = onehot(lane == (place_of(n) << 3) + 2 * (row >> 7) + (n & 1))
 
     pl.semaphore_wait(barrier, NX + NY - 2)
-    send(ST_B, "gy", t_b, r_b, False)
+    over_gy(lambda p: push(ST_B, t_b, r_b.at[place], p))
+    r_b[place] = t_b[...]
 
     row, lane = iota((256, 256), 0), iota((256, 256), 1)
     j, t = row >> 3, (row >> 2) & 1
@@ -195,8 +236,8 @@
 
     row, lane = iota((512, 128), 0), iota((512, 128), 1)
     s = row & 7
-    n = 2 * ((row >> 3) & 31) + (s & 1)
-    sel_g[...] = onehot((lane == ((n >> 2) << 3) + ((row >> 8) << 2) + (n & 3)) & (s < 6))
+    n = ((((row >> 4) & 7) + (((row >> 3) & 1) << 3)) << 2) + 2 * (core + (row >> 8) * (1 - 2 * core)) + (s & 1)
+    sel_g[...] = onehot((lane == ((n >> 2) << 3) + (((row >> 7) & 1) << 2) + (n & 3)) & (s < 6))
 
     lane_code, row_code = [], []
     id_rows = v_ids[...]
@@ -205,7 +246,7 @@
         a, b = iota((64, 64), 0), iota((64, 64), 1)
         column = jnp.sum(jnp.where(a == b, picked, 0.0), axis=1, keepdims=True)
         a, b = iota((64, 256), 0), iota((64, 256), 1)
-        of = 2 * (b >> 3) + (b & 1)
+        of = request_at(b)
         before = jnp.sum(jnp.where(a < of, column, 0.0), axis=0, keepdims=True)
         named = jnp.sum(jnp.where(a == of, column, 0.0), axis=0, keepdims=True)
         lane_code.append(jnp.where(named > 0.5, before, -1.0))
@@ -225,7 +266,7 @@
     sums_here = (
         ((q >> 1) == 0) & (slot == lane_code[0]) | ((q >> 1) == 1) & (slot == lane_code[1])
     ) & ((s >> 1) == 3)
-    own = ((q >> 1) == 2) & (lane == 8 * gy + 6 + (q & 1))
+    own = ((q >> 1) == 2) & (lane == 8 * place + 6 + (q & 1))
     perm_k[pl.ds(768, 128)] = onehot(sums_here | own)
 
     row, lane = iota((256, 256), 0), iota((256, 256), 1)
@@ -258,7 +299,7 @@
     sums = mm(left, v_wqkv[...])
     hh = (iota((128, 128), 0) >> 2) & 1
     sums = jnp.where(hh == 0, sums[:, 0:128], sums[:, 128:256])
-    s_c[...] = jnp.concatenate([sums.reshape(16, 8, 128), rows[384:512].reshape(16, 8, 128)], axis=1).astype(BF16)
+    s_c[...] = jnp.concatenate([sums.reshape(16, 8, 128), rows[384:512].reshape(16, 8, 128)], axis=1)
     send(ST_C, "gx", s_c, r_c, True)
     x_moe[...] = (x * mg).reshape(256, 128).astype(BF16)
     for c in loads[11:12]:
@@ -288,7 +329,7 @@
                 halves.append(pick(ct, [full[:, 128 * k : 128 * k + 128] for k in range(4)]).reshape(16, 8, 128))
             out[:, pl.ds(16 * e, 16), :] = jnp.concatenate(halves, axis=1).astype(BF16)
         sums = rows[768:896].reshape(16, 8, 128)
-        out[:, pl.ds(32, 16), :] = jnp.concatenate([sums, jnp.zeros((16, 8, 128), F32)], axis=1).astype(BF16)
+        out[:, pl.ds(32, 8), :] = sums.astype(BF16)
 
     gate_up(x_moe[...], s_a)
     send(ST_A, "gx", s_a, r_a, True)
@@ -338,7 +379,6 @@
     own_score = jnp.sum(own_query * fresh(24), axis=1, keepdims=True) * (HEAD_SIZE**-0.5 / CAP)
     own_weight = jnp.exp(CAP * jnp.tanh(own_score))
     own_value = own_weight.astype(BF16).astype(F32) * fresh(28)
-    total_a = None
 
     received(ST_E, r_e)
     tile = total(r_e)
@@ -354,24 +394,40 @@
 
     ctile = (iota((256, 128), 0) & 7) >> 1
     received(ST_F, r_f)
-    rows = mm(sel_g[...], r_f[...].astype(F32).reshape(128, 128).astype(BF16))
-    left = jnp.concatenate([rows[0:256], rows[256:512]], axis=1).astype(BF16)
-    sums = mm(left, v_wo[...])
-    s_g[...] = pick(ctile, [sums[:, 128 * c : 128 * c + 128] for c in range(3)]).reshape(32, 8, 128).astype(BF16)
-    send(ST_G, "gy", s_g, r_g, True)
+    heads16 = r_f[...].astype(F32).reshape(128, 128).astype(BF16)
+    cpair = (iota((128, 128), 0) & 7) >> 1
+
+    def project(other):
+        rows = mm(sel_g[pl.ds(256 * other, 256)], heads16).astype(BF16)
+        sums = mm(jnp.concatenate([rows[0:128], rows[128:256]], axis=1), v_wo[...])
+        return pick(cpair, [sums[:, 128 * c : 128 * c + 128] for c in range(3)]).reshape(8, 16, 128)
+
+    s_x[...] = project(1)
+    push(ST_X, s_x, r_x, 2 * z + 1 - core)
+    mine = project(0)
+    pltpu.make_async_copy(r_x, r_x, recv_sem.at[ST_X]).wait()
+    s_g[...] = (mine + r_x[...]).astype(BF16)
+    over_z(lambda far: push(ST_G, s_g.at[lax.rem(far, 8)], r_g.at[z], 2 * far + core))
+    r_g[z] = s_g[low_z]
     received(ST_A, r_a)
     total_a = total(r_a)
 
     received(ST_G, r_g)
-    branch = jnp.where(s8 < 6, total(r_g), 0.0)
-    gained = branch * pg
-    branch_t[...] = gained
-    branch_sums = lane_sums(
-        [(0, branch * branch), (1, base_t[...] * gained), (2, gained * gained)]
-        + [(3 + e, gained * rm[e]) for e in range(8)]
-    )
-    t_j[...] = jnp.where(s8 < 6, gained * mg, split_terms(branch_sums)).astype(BF16)
-    send(ST_J, "gy", t_j, r_j, False)
+    both = total(r_g)
+    tiles = []
+    for half in range(2):
+        branch = jnp.where(s8 < 6, both[8 * half : 8 * half + 8], 0.0)
+        gained = branch * pg
+        stream = jnp.where(s8 < 6, r_b[2 * pair + half].astype(F32), 0.0)
+        branch_sums = lane_sums(
+            [(0, branch * branch), (1, stream * gained), (2, gained * gained)]
+            + [(3 + e, gained * rm[e]) for e in range(8)]
+        )
+        tiles.append(jnp.where(s8 < 6, gained * mg, split_terms(branch_sums)))
+        branch_t[half] = gained
+    t_j[...] = jnp.concatenate(tiles, axis=0).astype(BF16)
+    over_near(lambda p: push(ST_J, t_j, r_j.at[pair], p))
+    r_j[pair] = t_j[...]
 
     received(ST_J, r_j)
     gate_up(r_j[...].astype(F32).reshape(256, 128).astype(BF16), s_k)
@@ -388,7 +444,6 @@
     exponent = jnp.where(named, jnp.exp(jnp.where(named, logits, 0.0)), 0.0)
     chance = exponent / jnp.sum(exponent, axis=1, keepdims=True)
     combine = jnp.sum(jnp.where(l8 == 3 + (s8 >> 1), chance, 0.0), axis=1, keepdims=True)
-    combine = combine.astype(BF16).astype(F32)
 
     def spread(column, first):
         two = [jnp.broadcast_to(column[first + k : first + k + 1], (8, 128)) for k in range(2)]
@@ -406,7 +461,7 @@
     t_h[...] = jnp.concatenate(hidden, axis=0).astype(BF16)
     send(ST_H, "gx", t_h, r_h, False)
 
-    mixed = as_rows(base_t[...] + spread(post, 4) * branch_t[...])
+    mixed = as_rows(base_t[...] + spread(post, 4) * branch_t[high])
 
     received(ST_H, r_h)
     hidden = r_h[...].astype(F32).reshape(256, 128).astype(BF16)
@@ -425,6 +480,7 @@
         (ST_K, r_k), (ST_H, r_h), (ST_L, r_l),
     ):
         pltpu.make_async_copy(peers_of(dst), peers_of(dst), send_sem.at[stage]).wait()
+    pltpu.make_async_copy(s_x, s_x, send_sem.at[ST_X]).wait()
 
 
 def local(
@@ -437,9 +493,10 @@
     gy_tiles = vmem((NY, 8, 128), BF16)
     gx_tiles = vmem((NX, 8, 128), BF16)
     tile = vmem((8, 128), BF16)
+    pairs = vmem((16, 16, 128), BF16)
     result = pl.pallas_call(
         kernel,
-        out_shape=jax.ShapeDtypeStruct((4, 384), BF16),
+        out_shape=pltpu.VMEM((4, 384), BF16),
         in_specs=[anywhere] * 5 + [scalars] * 2 + [anywhere] * 7,
         out_specs=pl.BlockSpec(memory_space=pltpu.VMEM),
         scratch_shapes=[
@@ -449,12 +506,13 @@
             vmem((2, 2, 384, 512), BF16),
             vmem((512, 256), BF16), vmem((256, 256), BF16), vmem((512, 128), BF16), vmem((896, 256), BF16),
             vmem((2048, 256), BF16), vmem((8, 8, 128), F32), vmem((8, 256), F32), vmem((8, 128), F32),
-            vmem((8, 128), F32), vmem((32, 8, 128), F32), vmem((256, 128), BF16),
-            tile, gy_tiles, vmem((NX, 16, 128), BF16), vmem((NX, 16, 128), BF16), tile, gy_tiles, gy_tiles, gy_tiles,
-            tile, gx_tiles, gy_tiles, gy_tiles, tile, gy_tiles, vmem((NX, 48, 128), BF16), vmem((NX, 48, 128), BF16),
-            vmem((NX, 48, 128), BF16), vmem((NX, 48, 128), BF16), vmem((16, 128), BF16), vmem((NX, 16, 128), BF16),
+            vmem((2, 8, 128), F32), vmem((32, 8, 128), F32), vmem((256, 128), BF16),
+            tile, gy_tiles, vmem((NX, 16, 128), F32), vmem((NX, 16, 128), F32), tile, gy_tiles, gy_tiles, gy_tiles,
+            tile, gx_tiles, vmem((8, 16, 128), F32), vmem((8, 16, 128), F32), vmem((8, 16, 128), BF16), pairs,
+            vmem((16, 128), BF16), pairs, vmem((NX, 40, 128), BF16), vmem((NX, 40, 128), BF16),
+            vmem((NX, 40, 128), BF16), vmem((NX, 40, 128), BF16), vmem((16, 128), BF16), vmem((NX, 16, 128), BF16),
             gy_tiles, gy_tiles,
-            pltpu.SemaphoreType.DMA((13,)), pltpu.SemaphoreType.DMA((11,)), pltpu.SemaphoreType.DMA((11,)),
+            pltpu.SemaphoreType.DMA((13,)), pltpu.SemaphoreType.DMA((12,)), pltpu.SemaphoreType.DMA((12,)),
         ],
         compiler_params=pltpu.CompilerParams(
             collective_id=0, has_side_effects=True, vmem_limit_bytes=63 * 1024 * 1024

time: 86.9 us -> 83.6 us (0.962)
  Pallas kernels: 84.7 us -> 82.3 us
    pallas_call x1, Pallas kernels: 84.7 us -> 82.3 us  [local(): pl.pallas_call(kernel, out_shape=pltpu.VMEM((4, 384), BF16), in_specs=[an...]
where the time goes in v3:
time: 83.6 us; the launch traced here: 83.5 us
  Pallas kernels  82.3 us (98%)
    pallas_call x1, Pallas kernels, local(): pl.pallas_call(kernel, out_shape=pltpu.VMEM((4, 384), BF16), in_specs=[an...  82.3 us

profile of v3, /device:TPU:1, one launch (start us, length us, event | category | flops | bytes accessed | tf_op | source)
XLA Modules:
  0.0 83.5 jit_solution(11437781145453284965)
XLA Ops:
  0.6 82.3 %decode_step.1 = bf16[4,384]{1,0:T(4,128)(2,1)S(1)} custom-call(bf16[2,384]{1,0:T(2,128)(2,1)} %residual.1, f32[384]{0:T(512)} %attn_gain.1, bf16[384,256]{1,0:T(8,128)(2,1)} %wqkv.1, bf16[4,64,1024]{2,1,0:T(8,128)(2,1)} %keys.1, bf16[4,64,1024]{2,1,0:T(8,128)(2,1)} %values.1, s32[4]{0:T(128)} %lengths.1, s32[4]{0:T(128)} %starts.1, bf16[192,384]{1,0:T(8,128)(2,1)} %wo.1, ...), custom_call_target="tpu_custom_call" | custom-call | tf_op jit(solution)/shard_map/decode_step/pallas_call | solution.py:497
  82.9 0.6 fusion

commit v4 on v3

--- a/solution.py
+++ b/solution.py
@@ -101,7 +101,7 @@
             act(2 * far + 1 - core)
             return carry
 
-        lax.fori_loop(0, 15, body, 0)
+        lax.fori_loop(0, 15, body, 0, unroll=True)
         act(2 * z + 1 - core)
 
     def over_gx(act):
@@ -114,7 +114,7 @@
             act(4 * qx + qy)
             return carry
 
-        lax.fori_loop(0, 15, body, 0)
+        lax.fori_loop(0, 15, body, 0, unroll=True)
 
     barrier = pltpu.get_barrier_semaphore()
     over_gy(lambda p: pl.semaphore_signal(barrier, inc=1, device_id=(gx, p), device_id_type=MESH))
@@ -167,7 +167,7 @@
             act(lax.rem(z + 8 + h * (1 - 2 * lax.rem(q, 2)), 16))
             return carry
 
-        lax.fori_loop(0, 15, body, 0)
+        lax.fori_loop(0, 15, body, 0, unroll=True)
 
     def over_near(act):
         def body(q, carry):
@@ -177,7 +177,7 @@
             act(2 * near + 1 - core)
             return carry
 
-        lax.fori_loop(0, 7, body, 0)
+        lax.fori_loop(0, 7, body, 0, unroll=True)
         act(2 * z + 1 - core)
 
     def push(stage, src, dst, p):
@@ -251,7 +251,7 @@
         named = jnp.sum(jnp.where(a == of, column, 0.0), axis=0, keepdims=True)
         lane_code.append(jnp.where(named > 0.5, before, -1.0))
         a, b = iota((256, 64), 0), iota((256, 64), 1)
-        of = 2 * (a >> 3) + (a & 1)
+        of = 4 * ((z + 5 + (a >> 4)) & 15) + 2 * ((a >> 3) & 1) + (a & 1)
         before = jnp.sum(jnp.where(b < of, picked, 0.0), axis=1, keepdims=True)
         named = jnp.sum(jnp.where(b == of, picked, 0.0), axis=1, keepdims=True)
         row_code.append(jnp.where(named > 0.5, before, -1.0))
@@ -274,7 +274,9 @@
     for e in range(EXP_WIN):
         here = (slot == row_code[e]) & (((lane >> 3) & 1) == e) & ((row & 7) < 6)
         for ct in range(4):
-            perm_l[pl.ds((4 * e + ct) * 256, 256)] = onehot(here & (((lane >> 1) & 3) == ct))
+            block = onehot(here & (((lane >> 1) & 3) == ct))
+            for part in range(2):
+                perm_l[pl.ds(1024 * part + 512 * e + 128 * ct, 128)] = block[128 * part : 128 * part + 128]
 
     row, lane = iota((8, 256), 0), iota((8, 256), 1)
     last = pick(lane >> 6, [lengths[r] for r in range(4)]) - 1
@@ -465,13 +467,41 @@
 
     received(ST_H, r_h)
     hidden = r_h[...].astype(F32).reshape(256, 128).astype(BF16)
-    sums = jnp.zeros((256, 384), F32)
-    for e in range(EXP_WIN):
-        rows = mm(perm_l[pl.ds(1024 * e, 1024)], hidden).astype(BF16)
-        left = jnp.concatenate([rows[256 * ct : 256 * ct + 256] for ct in range(4)], axis=1)
-        sums = sums + mm(left, v_wd[e])
-    s_l[...] = pick(ctile, [sums[:, 128 * c : 128 * c + 128] for c in range(3)]).reshape(32, 8, 128).astype(BF16)
-    send(ST_L, "gy", s_l, r_l, True)
+    chalf = (iota((128, 128), 0) & 7) >> 1
+
+    def expert_sums(part):
+        sums = jnp.zeros((128, 384), F32)
+        for e in range(EXP_WIN):
+            rows = mm(perm_l[pl.ds(1024 * part + 512 * e, 512)], hidden).astype(BF16)
+            left = jnp.concatenate([rows[128 * ct : 128 * ct + 128] for ct in range(4)], axis=1)
+            sums = sums + mm(left, v_wd[e])
+        blocks = pick(chalf, [sums[:, 128 * c : 128 * c + 128] for c in range(3)])
+        s_l[pl.ds(16 * part, 16)] = blocks.reshape(16, 8, 128).astype(BF16)
+
+    def send_sums(k):
+        chip = lax.rem(z + 5 + k, 16)
+        for other in range(2):
+            push(ST_L, s_l.at[2 * k + other], r_l.at[gy], 2 * chip + other)
+
+    expert_sums(0)
+
+    def far_chips(q, carry):
+        h = lax.div(q + 1, 2)
+        send_sums(3 + h * (1 - 2 * lax.rem(q, 2)))
+        return carry
+
+    lax.fori_loop(0, 7, far_chips, 0, unroll=True)
+    send_sums(7)
+    expert_sums(1)
+
+    def near_chips(k, carry):
+        send_sums(k)
+        return carry
+
+    lax.fori_loop(8, 11, near_chips, 0, unroll=True)
+    lax.fori_loop(12, 16, near_chips, 0, unroll=True)
+    push(ST_L, s_l.at[23 - core], r_l.at[gy], 2 * z + 1 - core)
+    r_l[gy] = s_l[22 + core]
     received(ST_L, r_l)
     res_ref[...] = jnp.concatenate([mixed, as_rows(total(r_l))], axis=0).astype(BF16)
 

time: 83.6 us -> 82.8 us (level)
  no operation moved by 1% of the time
where the time goes in v4:
time: 82.8 us; the launch traced here: 82.7 us
  Pallas kernels  81.5 us (98%)
    pallas_call x1, Pallas kernels, local(): pl.pallas_call(kernel, out_shape=pltpu.VMEM((4, 384), BF16), in_specs=[an...  81.5 us

profile of v4, /device:TPU:1, one launch (start us, length us, event | category | flops | bytes accessed | tf_op | source)
XLA Modules:
  0.0 82.7 jit_solution(7208466724884504295)
XLA Ops:
  0.6 81.5 %decode_step.1 = bf16[4,384]{1,0:T(4,128)(2,1)S(1)} custom-call(bf16[2,384]{1,0:T(2,128)(2,1)} %residual.1, f32[384]{0:T(512)} %attn_gain.1, bf16[384,256]{1,0:T(8,128)(2,1)} %wqkv.1, bf16[4,64,1024]{2,1,0:T(8,128)(2,1)} %keys.1, bf16[4,64,1024]{2,1,0:T(8,128)(2,1)} %values.1, s32[4]{0:T(128)} %lengths.1, s32[4]{0:T(128)} %starts.1, bf16[192,384]{1,0:T(8,128)(2,1)} %wo.1, ...), custom_call_target="tpu_custom_call" | custom-call | tf_op jit(solution)/shard_map/decode_step/pallas_call | solution.py:527
  82.1 0.6 fusion

commit v5 on v4

--- a/solution.py
+++ b/solution.py
@@ -81,7 +81,7 @@
     residual, attn_gain, wqkv, keys, values, lengths, starts, wo, post_gain, moe_gain, router, ids, w_gate_up, w_down,
     res_ref,
     v_res, v_ag, v_pg, v_mg, v_rt, v_ids, v_wqkv, v_keys, v_vals, v_wo, v_gu, v_wd, w_split,
-    perm_c, sel_e, sel_g, perm_k, perm_l, rm, mask, base_t, branch_t, q_rows, x_moe,
+    perm_c, sel_e, sel_g, perm_k, perm_l, rm, mask, base_t, branch_t, q_rows, q_bits, x_moe,
     t_b, r_b, s_c, r_c, t_d, r_d, s_e, r_e, t_f, r_f, s_x, r_x, s_g, r_g, t_j, r_j, s_a, r_a, s_k, r_k, t_h, r_h, s_l, r_l,
     load_sem, send_sem, recv_sem,
 ):
@@ -343,32 +343,58 @@
     queries = mm(sel_e[...], everything)
     q_rows[...] = queries.reshape(32, 8, 128)
     queries = queries.astype(BF16)
-    scores = []
-    for g in range(KEY_VALUE_HEADS):
-        kg = v_keys[:, :, pl.ds(128 * g, 128)].reshape(256, 128)
-        scores.append(
-            lax.dot_general(
-                queries[32 * g : 32 * g + 32], kg, (((1,), (1,)), ((), ())), preferred_element_type=F32
+    q_bits[...] = queries
+
+    def attend(part):
+        groups = [lax.rem(lax.div(z, 2) + 2 + 4 * part + k, 8) for k in range(4)]
+        scores = []
+        for g in groups:
+            lanes = pl.ds(pl.multiple_of(128 * g, 128), 128)
+            scores.append(
+                lax.dot_general(
+                    q_bits[pl.ds(pl.multiple_of(32 * g, 32), 32)],
+                    v_keys[:, :, lanes].reshape(256, 128),
+                    (((1,), (1,)), ((), ())),
+                    preferred_element_type=F32,
+                )
             )
-        )
-    score = jnp.concatenate(scores, axis=0)
-    weight = jnp.exp(CAP * jnp.tanh(score * (HEAD_SIZE**-0.5 / CAP))).reshape(32, 8, 256) * mask[...]
-    weight = weight.reshape(256, 256)
-    weight16 = weight.astype(BF16)
-    sums = []
-    for g in range(KEY_VALUE_HEADS):
-        vg = v_vals[:, :, pl.ds(128 * g, 128)].reshape(256, 128)
-        sums.append(mm(weight16[32 * g : 32 * g + 32], vg))
-    summed = jnp.concatenate(sums, axis=0)
-    total1 = jnp.broadcast_to(jnp.sum(weight, axis=1, keepdims=True), (256, 128))
-    total0 = pltpu.roll(total1, 4, 0)
-    row, lane = iota((256, 128), 0), iota((256, 128), 1)
-    low1 = total1 - total1.astype(BF16).astype(F32)
-    low0 = total0 - total0.astype(BF16).astype(F32)
-    free = pick((lane & 63) >> 4, [total1, low1, total0, low0])
-    keep = (((row >> 2) & 1) == 0) | ((lane >> 6) == ((row >> 3) & 1))
-    s_e[...] = jnp.where(keep, summed, free).reshape(32, 8, 128).astype(BF16)
-    send(ST_E, "gy", s_e, r_e, True)
+        score = jnp.concatenate(scores, axis=0)
+        weight = jnp.exp(CAP * jnp.tanh(score * (HEAD_SIZE**-0.5 / CAP))).reshape(16, 8, 256) * mask[...]
+        weight = weight.reshape(128, 256)
+        weight16 = weight.astype(BF16)
+        sums = []
+        for k, g in enumerate(groups):
+            lanes = pl.ds(pl.multiple_of(128 * g, 128), 128)
+            sums.append(mm(weight16[32 * k : 32 * k + 32], v_vals[:, :, lanes].reshape(256, 128)))
+        summed = jnp.concatenate(sums, axis=0)
+        total1 = jnp.broadcast_to(jnp.sum(weight, axis=1, keepdims=True), (128, 128))
+        total0 = pltpu.roll(total1, 4, 0)
+        row, lane = iota((128, 128), 0), iota((128, 128), 1)
+        low1 = total1 - total1.astype(BF16).astype(F32)
+        low0 = total0 - total0.astype(BF16).astype(F32)
+        free = pick((lane & 63) >> 4, [total1, low1, total0, low0])
+        keep = (((row >> 2) & 1) == 0) | ((lane >> 6) == ((row >> 3) & 1))
+        s_e[pl.ds(16 * part, 16)] = jnp.where(keep, summed, free).reshape(16, 8, 128).astype(BF16)
+
+    first_chip = 2 * lax.div(z, 2) + 4
+
+    def send_attended(k):
+        chip = lax.rem(first_chip + k, 16)
+        for c in range(2):
+            push(ST_E, s_e.at[2 * k + c], r_e.at[gy], 2 * chip + c)
+
+    attend(0)
+    for k in (4, 3, 5, 2, 6, 1, 7, 0):
+        send_attended(k)
+    attend(1)
+    for k in (8, 15, 9, 14, 10, 11):
+        send_attended(k)
+    beside = 1 - lax.rem(z, 2)
+    for c in range(2):
+        push(ST_E, s_e.at[24 + 2 * beside + c], r_e.at[gy], 2 * (2 * lax.div(z, 2) + beside) + c)
+    own_block = 24 + 2 * lax.rem(z, 2)
+    push(ST_E, s_e.at[own_block + 1 - core], r_e.at[gy], 2 * z + 1 - core)
+    r_e[gy] = s_e[own_block + core]
 
     group = lax.div(gy, 4)
     second = lax.rem(group, 2)
@@ -502,15 +528,15 @@
     lax.fori_loop(12, 16, near_chips, 0, unroll=True)
     push(ST_L, s_l.at[23 - core], r_l.at[gy], 2 * z + 1 - core)
     r_l[gy] = s_l[22 + core]
-    received(ST_L, r_l)
-    res_ref[...] = jnp.concatenate([mixed, as_rows(total(r_l))], axis=0).astype(BF16)
-
     for stage, dst in (
         (ST_B, r_b), (ST_C, r_c), (ST_D, r_d), (ST_E, r_e), (ST_F, r_f), (ST_G, r_g), (ST_J, r_j), (ST_A, r_a),
-        (ST_K, r_k), (ST_H, r_h), (ST_L, r_l),
+        (ST_K, r_k), (ST_H, r_h),
     ):
         pltpu.make_async_copy(peers_of(dst), peers_of(dst), send_sem.at[stage]).wait()
     pltpu.make_async_copy(s_x, s_x, send_sem.at[ST_X]).wait()
+    received(ST_L, r_l)
+    res_ref[...] = jnp.concatenate([mixed, as_rows(total(r_l))], axis=0).astype(BF16)
+    pltpu.make_async_copy(peers_of(r_l), peers_of(r_l), send_sem.at[ST_L]).wait()
 
 
 def local(
@@ -536,7 +562,7 @@
             vmem((2, 2, 384, 512), BF16),
             vmem((512, 256), BF16), vmem((256, 256), BF16), vmem((512, 128), BF16), vmem((896, 256), BF16),
             vmem((2048, 256), BF16), vmem((8, 8, 128), F32), vmem((8, 256), F32), vmem((8, 128), F32),
-            vmem((2, 8, 128), F32), vmem((32, 8, 128), F32), vmem((256, 128), BF16),
+            vmem((2, 8, 128), F32), vmem((32, 8, 128), F32), vmem((256, 128), BF16), vmem((256, 128), BF16),
             tile, gy_tiles, vmem((NX, 16, 128), F32), vmem((NX, 16, 128), F32), tile, gy_tiles, gy_tiles, gy_tiles,
             tile, gx_tiles, vmem((8, 16, 128), F32), vmem((8, 16, 128), F32), vmem((8, 16, 128), BF16), pairs,
             vmem((16, 128), BF16), pairs, vmem((NX, 40, 128), BF16), vmem((NX, 40, 128), BF16),

time: 82.8 us -> 82.7 us (level)
  no operation moved by 1% of the time
where the time goes in v5:
time: 82.7 us; the launch traced here: 82.6 us
  Pallas kernels  81.4 us (98%)
    pallas_call x1, Pallas kernels, local(): pl.pallas_call(kernel, out_shape=pltpu.VMEM((4, 384), BF16), in_specs=[an...  81.4 us

profile of v5, /device:TPU:1, one launch (start us, length us, event | category | flops | bytes accessed | tf_op | source)
XLA Modules:
  0.0 82.6 jit_solution(14746569655538323318)
XLA Ops:
  0.6 81.4 %decode_step.1 = bf16[4,384]{1,0:T(4,128)(2,1)S(1)} custom-call(bf16[2,384]{1,0:T(2,128)(2,1)} %residual.1, f32[384]{0:T(512)} %attn_gain.1, bf16[384,256]{1,0:T(8,128)(2,1)} %wqkv.1, bf16[4,64,1024]{2,1,0:T(8,128)(2,1)} %keys.1, bf16[4,64,1024]{2,1,0:T(8,128)(2,1)} %values.1, s32[4]{0:T(128)} %lengths.1, s32[4]{0:T(128)} %starts.1, bf16[192,384]{1,0:T(8,128)(2,1)} %wo.1, ...), custom_call_target="tpu_custom_call" | custom-call | tf_op jit(solution)/shard_map/decode_step/pallas_call | solution.py:553
  82.0 0.6 fusion
